TPU v7x, 512 devices: a whole 4x8x8 slice. The times are simulated.
512 devices in a mesh: dp: 8 (over z), tensor: 4 (over y_lo, core), grid: 16 (over y_hi, x).
Axes of the slice: x: 4, y: 8 (y_hi: 4, y_lo: 2; y = y_hi * 2 + y_lo), z: 8, core: 2. Of those that a mesh axis runs over, the one named last changes fastest.
Arguments:
- tokens: bfloat16 [6144, 8192], P('dp', 'grid'), may hold values from -6 to 6
- cotangents: bfloat16 [2, 6144, 1024], P(None, 'dp', 'tensor'), may hold values from -0.015625 to 0.015625
- left_stat: float32 [2, 8192, 8192], P(None, ('dp', 'tensor'), 'grid'), may hold values from -6 to 6
- right_stat: float32 [2, 1024, 1024], P(None, ('dp', 'tensor'), 'grid'), may hold values from -6 to 6
- left_root: bfloat16 [2, 8192, 8192], P(None, ('dp', 'tensor'), 'grid'), may hold values from -0.3125 to 0.3125
- right_root: bfloat16 [2, 1024, 1024], P(None, 'grid'), as said below
- momentum: float32 [2, 8192, 1024], P(None, ('dp', 'tensor', 'grid')), may hold values from -6 to 6
Outputs:
- new_left: float32 [2, 8192, 8192], P(None, ('dp', 'tensor'), 'grid')
- new_right: float32 [2, 1024, 1024], P(None, ('dp', 'tensor'), 'grid')
- new_momentum: float32 [2, 8192, 1024], P(None, ('dp', 'tensor', 'grid'))
Inputs may be any that keep to these rules, and one draw needn't show every extreme that they name: `right_root`: each of the two factors is exactly symmetric.
All inputs are finite; a program needn't handle non-finite values.
Results may differ from a plain program's by a relative error of at most 0.0023.
Values may be sent and summed in bfloat16 or wider, within the bound.
A program may use at most 64 MiB of HBM per device.

v0:
```python
import jax
import jax.numpy as jnp
from jax import lax
from jax.sharding import PartitionSpec as P

stat_decay = 0.9
momentum_decay = 0.9


def in_blocks(shard, dim, size):
    dims = shard.shape
    pieces = shard.reshape(*dims[:dim], size, dims[dim] // size, *dims[dim + 1 :])
    return jnp.moveaxis(pieces, dim, 0)


def sum_at_owner(shard, axis, dim):
    size = lax.axis_size(axis)
    pieces = lax.all_to_all(in_blocks(shard, dim, size), axis, 0, 0, tiled=True)
    return jnp.sum(pieces, axis=0)


def rows_for(lines, size):
    spare = -lines.shape[0] % size
    if not spare:
        return lines
    return jnp.concatenate([lines, jnp.zeros((spare, *lines.shape[1:]), lines.dtype)])


def spread(shard, axis, root):
    lines = jnp.where(lax.axis_index(axis) == root, shard, jnp.zeros_like(shard)).reshape(
        -1, *shard.shape[1:][-1:]
    )
    padded = rows_for(lines, lax.axis_size(axis))
    own = lax.psum_scatter(padded, axis, scatter_dimension=0, tiled=True)
    return lax.all_gather(own, axis, axis=0, tiled=True)[: len(lines)].reshape(shard.shape)


def shards(tokens, cotangents, left_stat, right_stat, left_root, right_root, momentum):
    partial_grad = jnp.einsum("tr,pto->pro", tokens, cotangents, preferred_element_type=jnp.float32)
    shared = sum_at_owner(partial_grad, "dp", 1)
    widened = lax.all_gather(shared.astype(jnp.bfloat16), "tensor", axis=2, tiled=True)
    grad_rows = lax.all_gather(widened, "dp", axis=1, tiled=True)
    block_rows = left_stat.shape[1]
    grid_rows = left_stat.shape[2]
    learner = lax.axis_index("dp") * lax.axis_size("tensor") + lax.axis_index("tensor")
    first_row = learner * block_rows
    source = first_row // grid_rows
    offset = first_row % grid_rows
    selected = lax.dynamic_slice_in_dim(grad_rows, offset, block_rows, 1)
    own_rows = spread(selected, "grid", source)
    gram_left = jnp.einsum("pak,pbk->pab", own_rows, grad_rows, preferred_element_type=jnp.float32)
    new_left = stat_decay * left_stat + (1.0 - stat_decay) * gram_left
    column_width = right_stat.shape[2]
    column_block = lax.dynamic_slice_in_dim(
        own_rows, lax.axis_index("grid") * column_width, column_width, 2
    )
    right_term = jnp.einsum(
        "pak,pac->pkc", own_rows, column_block, preferred_element_type=jnp.float32
    )
    gram_right = sum_at_owner(right_term, ("dp", "tensor"), 1)
    new_right = stat_decay * right_stat + (1.0 - stat_decay) * gram_right
    applied = sum_at_owner(
        jnp.einsum("pab,pbk->apk", left_root, grad_rows, preferred_element_type=jnp.float32),
        "grid",
        0,
    )
    factor_local = right_root.astype(jnp.float32)
    local_columns = jnp.einsum(
        "mpk,pck->mpc",
        lax.all_gather(applied, "grid", axis=0, tiled=True),
        factor_local,
        precision=lax.Precision.HIGHEST,
        preferred_element_type=jnp.float32,
    )
    update = lax.all_to_all(local_columns, "grid", split_axis=0, concat_axis=2, tiled=True)
    new_momentum = momentum_decay * momentum + jnp.transpose(update, (1, 0, 2))
    return (new_left, new_right, new_momentum)


def solution(mesh):
    return jax.shard_map(
        shards,
        mesh=mesh,
        in_specs=(
            P("dp", "grid"),
            P(None, "dp", "tensor"),
            P(None, ("dp", "tensor"), "grid"),
            P(None, ("dp", "tensor"), "grid"),
            P(None, ("dp", "tensor"), "grid"),
            P(None, "grid", None),
            P(None, ("dp", "tensor", "grid"), None),
        ),
        out_specs=(
            P(None, ("dp", "tensor"), "grid"),
            P(None, ("dp", "tensor"), "grid"),
            P(None, ("dp", "tensor", "grid"), None),
        ),
        check_vma=False,
    )
```

profile of v0, /device:TPU:8, one launch (start us, length us, event | category | flops | bytes accessed | tf_op | source)
XLA Modules:
  0.0 374.3 jit_solution(8418410943962718748)
XLA Ops:
  7.2 0.0 copy-start
  7.2 0.0 all-gather.4.cloned.1.call-start
  7.2 1.1 copy-done
  8.3 1.7 convolution_bitcast_fusion
  10.0 0.3 copy.25
  10.4 0.1 copy.26
  10.5 38.8 %all_to_all.33 = f32[8,2,64,256]{3,2,1,0:T(8,128)S(1)} all-to-all(f32[8,2,64,256]{3,2,1,0:T(8,128)S(1)} %copy.26), channel_id=1, replica_groups=mesh['dp'=8,'tensor'=4,'grid'=16] {'dp'}, dimensions={0} | all-to-all | bytes 2097152 | tf_op jit(solution)/shard_map/all_to_all | solution.py:18
  49.3 0.1 reduce_sum.27
  49.4 0.0 copy-start.2
  49.4 6.4 %all_gather.12 = bf16[2,64,1024]{2,1,0:T(8,128)(2,1)} all-gather(bf16[2,64,256]{2,1,0:T(8,128)(2,1)S(1)} %reduce_sum.27), channel_id=1, replica_groups=mesh['dp'=8,'tensor'=4,'grid'=16] {'tensor'}, dimensions={2}, use_global_device_ids=true | all-gather | bytes 327680 | tf_op jit(solution)/shard_map/all_gather | solution.py:41
  55.8 0.0 all-gather.4.cloned.1.call-update
  55.8 0.0 reduce-scatter.2.cloned.1.call-start
  55.9 40.9 %all-gather.4.cloned.1.call-done = bf16[2,512,1024]{2,1,0:T(8,128)(2,1)} async-done(((bf16[2,64,1024]{2,1,0:T(8,128)(2,1)}), bf16[2,512,1024]{2,1,0:T(8,128)(2,1)}) %all-gather.4.cloned.1.call-update) | async-done | bytes 2097168 | tf_op jit(solution)/shard_map/all_gather | solution.py:42
  96.8 0.0 copy-start.1
  96.8 2.6 dynamic-slice_select_fusion
  99.3 0.0 reduce-scatter.2.cloned.1.call-update
  99.4 0.0 copy-done.2
  99.4 0.0 copy-done.1
  99.4 0.7 fusion.5
  100.1 1.4 copy.30
  101.5 8.4 %all-to-all-start.2 = ((f32[16,16,2,1024]{3,1,2,0:T(8,128)}), f32[16,16,2,1024]{3,1,2,0:T(8,128)}, u32[]{:S(2)}, u32[]{:S(2)}) async-start(f32[16,16,2,1024]{3,1,2,0:T(8,128)} %copy.30), calls=%async_computation.3 | async-start | bytes 4194304 | tf_op jit(solution)/shard_map/all_to_all | solution.py:18
  110.0 0.0 all-gather.6.cloned.1.call-start
  110.0 108.0 %reduce-scatter.2.cloned.1.call-done = bf16[32,1024]{1,0:T(8,128)(2,1)} async-done(((bf16[512,1024]{1,0:T(8,128)(2,1)}), bf16[32,1024]{1,0:T(8,128)(2,1)}) %reduce-scatter.2.cloned.1.call-update) | async-done | bytes 65552 | tf_op jit(solution)/shard_map/reduce_scatter | solution.py:34
  218.0 0.0 all-gather.6.cloned.1.call-update
  218.0 0.0 all-gather.8.cloned.1.call-start
  218.0 0.0 all-to-all-done.2
  218.0 2.4 reduce_sum.29
  220.4 0.0 all-gather.8.cloned.1.call-update
  220.4 57.0 %all-gather.6.cloned.1.call-done = bf16[512,1024]{1,0:T(8,128)(2,1)} async-done(((bf16[32,1024]{1,0:T(8,128)(2,1)}), bf16[512,1024]{1,0:T(8,128)(2,1)}) %all-gather.6.cloned.1.call-update) | async-done | bytes 1048592 | tf_op jit(solution)/shard_map/all_gather | solution.py:35
  277.4 1.8 fusion.2
  279.3 1.1 copy.29
  280.3 2.7 reshape.27
  283.0 9.3 %all-to-all-start.1 = ((f32[32,1,4096]{2,1,0:T(1,128)}), f32[32,1,4096]{2,1,0:T(1,128)S(1)}, u32[]{:S(2)}, u32[]{:S(2)}) async-start(f32[32,1,4096]{2,1,0:T(1,128)} %reshape.27), calls=%async_computation.2 | async-start | bytes 1048576 | tf_op jit(solution)/shard_map/all_to_all | solution.py:18
  292.4 50.8 %all-gather.8.cloned.1.call-done = f32[256,2,1024]{2,0,1:T(8,128)} async-done(((f32[16,2,1024]{2,0,1:T(8,128)}), f32[256,2,1024]{2,0,1:T(8,128)}) %all-gather.8.cloned.1.call-update) | async-done | bytes 2097168 | tf_op jit(solution)/shard_map/all_gather | solution.py:70
  343.1 2.8 convolution_bitcast_fusion.1
  345.9 0.8 copy.31
  346.8 1.9 reshape.29
  348.6 0.0 all-to-all-done.1
  348.6 6.7 %all-to-all-start.3 = ((f32[16,1,2048]{2,1,0:T(1,128)}), f32[16,1,2048]{2,1,0:T(1,128)S(1)}, u32[]{:S(2)}, u32[]{:S(2)}) async-start(f32[16,1,2048]{2,1,0:T(1,128)} %reshape.29), calls=%async_computation.4 | async-start | bytes 262144 | tf_op jit(solution)/shard_map/all_to_all | solution.py:75
  355.4 3.3 fusion
  358.7 0.0 copy-start.4
  358.7 0.5 broadcast.2
  359.2 1.8 reduce
  361.0 0.0 copy-start.3
  361.0 0.4 reshape.28
  361.4 0.1 reduce_sum.28
  361.5 0.0 copy-done.4
  361.5 0.6 multiply_add_fusion
  362.1 3.6 all-to-all-done.3
  365.8 0.9 reduce.1
  366.6 0.2 reshape.30
  366.8 0.1 copy.33
  366.9 0.1 all_to_all.28
  367.1 0.0 copy-done.3
  367.1 0.7 bitcast_add_fusion
  (1 shorter events, 0.0 us)
Async XLA Ops:
  7.2 1.1 copy-start
  7.2 89.6 %all-gather.4.cloned.1.call-start = ((), (), s32[]{:S(2)}) async-start(), calls=%async_computation.5 | async-start | bytes 2359296 | tf_op jit(solution)/shard_map/all_gather | solution.py:42
  49.4 50.0 %copy-start.2 = (bf16[2,256,512]{2,1,0:T(8,128)(2,1)S(1)}, bf16[2,256,512]{2,1,0:T(8,128)(2,1)}, u32[]{:S(2)}) copy-start(bf16[2,256,512]{2,1,0:T(8,128)(2,1)} %param.11) | copy-start | bytes 1572868
  55.8 162.1 %reduce-scatter.2.cloned.1.call-start = ((), (), s32[]{:S(2)}) async-start(), calls=%async_computation.6 | async-start | bytes 1114112 | tf_op jit(solution)/shard_map/reduce_scatter | solution.py:34
  96.8 2.6 copy-start.1
  101.5 116.5 %all-to-all-start.2 = ((f32[16,16,2,1024]{3,1,2,0:T(8,128)}), f32[16,16,2,1024]{3,1,2,0:T(8,128)}, u32[]{:S(2)}, u32[]{:S(2)}) async-start(f32[16,16,2,1024]{3,1,2,0:T(8,128)} %copy.30), calls=%async_computation.3 | async-start | bytes 4194304 | tf_op jit(solution)/shard_map/all_to_all | solution.py:18
  110.0 167.5 %all-gather.6.cloned.1.call-start = ((), (), s32[]{:S(2)}) async-start(), calls=%async_computation.7 | async-start | bytes 1114112 | tf_op jit(solution)/shard_map/all_gather | solution.py:35
  218.0 125.2 %all-gather.8.cloned.1.call-start = ((), (), s32[]{:S(2)}) async-start(), calls=%async_computation.8 | async-start | bytes 2228224 | tf_op jit(solution)/shard_map/all_gather | solution.py:70
  283.0 65.6 %all-to-all-start.1 = ((f32[32,1,4096]{2,1,0:T(1,128)}), f32[32,1,4096]{2,1,0:T(1,128)S(1)}, u32[]{:S(2)}, u32[]{:S(2)}) async-start(f32[32,1,4096]{2,1,0:T(1,128)} %reshape.27), calls=%async_computation.2 | async-start | bytes 1048576 | tf_op jit(solution)/shard_map/all_to_all | solution.py:18
  348.6 17.1 %all-to-all-start.3 = ((f32[16,1,2048]{2,1,0:T(1,128)}), f32[16,1,2048]{2,1,0:T(1,128)S(1)}, u32[]{:S(2)}, u32[]{:S(2)}) async-start(f32[16,1,2048]{2,1,0:T(1,128)} %reshape.29), calls=%async_computation.4 | async-start | bytes 262144 | tf_op jit(solution)/shard_map/all_to_all | solution.py:75
  358.7 2.9 copy-start.4
  361.0 6.1 %copy-start.3 = (f32[2,16,1024]{2,1,0:T(8,128)S(1)}, f32[2,16,1024]{2,1,0:T(8,128)}, u32[]{:S(2)}) copy-start(f32[2,16,1024]{2,1,0:T(8,128)} %param.13) | copy-start | bytes 393220
Sparse Core Ops, SparseCore 0:
  55.9 40.7 all-gather.3
  101.4 116.5 reduce-scatter.1
  221.4 55.9 all-gather.5
  281.3 61.7 all-gather.7
where the time goes:
time: 375 us; the launch traced here: 374 us
  waiting for transfers between devices  260 us (69%)
  blocking collectives  45.2 us (12%)
  starting transfers between devices  24.6 us (7%)
  between operations  14 us (4%)
  local copies, waits for them, and re-layouts  10.7 us (3%)
  matrix products  10.4 us (3%)
  other arithmetic  9.07 us (2%)
    reduce_scatter x1, waiting for transfers between devices, spread(): own = lax.psum_scatter(padded, axis, scatter_dimension=0, tiled=True)  108 us
    all_gather x1, waiting for transfers between devices, spread(): lax.all_gather(own, axis, axis=0, tiled=True)[:len(lines)]  57 us
    all_gather x1, waiting for transfers between devices, shards(): lax.all_gather(applied, 'grid', axis=0, tiled=True)  50.8 us
    all_gather x1, waiting for transfers between devices, shards(): grad_rows = lax.all_gather(widened, 'dp', axis=1, tiled=True)  40.9 us
    all_to_all x1, blocking collectives, sum_at_owner(): pieces = lax.all_to_all(in_blocks(shard, dim, size), axis, 0, 0, tiled=True)  38.8 us
    all_to_all x2, starting transfers between devices, sum_at_owner(): pieces = lax.all_to_all(in_blocks(shard, dim, size), axis, 0, 0, tiled=True)  17.8 us
  transfers between devices with their start and end apart: 7, of which 5 were waited for; matrix products, arithmetic and copies ran while one was open for 6% of the time, Pallas kernels for 0%

commit v1 on v0

--- a/solution.py
+++ b/solution.py
@@ -1,3 +1,4 @@
+import functools
 import jax
 import jax.numpy as jnp
 from jax import lax
@@ -5,6 +6,15 @@
 
 stat_decay = 0.9
 momentum_decay = 0.9
+
+
+def loads_turn(message, dimension_no):
+    return jnp.concatenate(
+        lax.all_to_all(jnp.stack(lax.axis_size("dp") * [message], 0), "dp", 0, 0), dimension_no
+    )
+
+
+draw_skins_in = functools.partial(loads_turn, dimension_no=1)
 
 
 def in_blocks(shard, dim, size):
@@ -39,7 +49,7 @@
     partial_grad = jnp.einsum("tr,pto->pro", tokens, cotangents, preferred_element_type=jnp.float32)
     shared = sum_at_owner(partial_grad, "dp", 1)
     widened = lax.all_gather(shared.astype(jnp.bfloat16), "tensor", axis=2, tiled=True)
-    grad_rows = lax.all_gather(widened, "dp", axis=1, tiled=True)
+    grad_rows = draw_skins_in(widened)
     block_rows = left_stat.shape[1]
     grid_rows = left_stat.shape[2]
     learner = lax.axis_index("dp") * lax.axis_size("tensor") + lax.axis_index("tensor")

time: 375 us -> 390 us (1.040)
  waiting for transfers between devices: 260 us -> 268 us
  local copies, waits for them, and re-layouts: 10.7 us -> 15.6 us
  starting transfers between devices: 24.6 us -> 28.6 us
    all_to_all x0 -> x1, waiting for transfers between devices: none -> 51.9 us  [loads_turn(): lax.all_to_all(jnp.stack(lax.axis_size('dp') * [message], 0), 'dp', 0, 0)]
    all_gather x1 -> x0, waiting for transfers between devices: 40.9 us -> none  [shards(): grad_rows = lax.all_gather(widened, 'dp', axis=1, tiled=True)]
where the time goes in v1:
time: 390 us; the launch traced here: 389 us
  waiting for transfers between devices  268 us (69%)
  blocking collectives  44.6 us (11%)
  starting transfers between devices  28.6 us (7%)
  local copies, waits for them, and re-layouts  15.6 us (4%)
  between operations  14 us (4%)
  matrix products  10.4 us (3%)
  other arithmetic  7.81 us (2%)
    reduce_scatter x1, waiting for transfers between devices, spread(): own = lax.psum_scatter(padded, axis, scatter_dimension=0, tiled=True)  105 us
    all_gather x1, waiting for transfers between devices, spread(): lax.all_gather(own, axis, axis=0, tiled=True)[:len(lines)]  57 us
    all_to_all x1, waiting for transfers between devices, loads_turn(): lax.all_to_all(jnp.stack(lax.axis_size('dp') * [message], 0), 'dp', 0, 0)  51.9 us
    all_gather x1, waiting for transfers between devices, shards(): lax.all_gather(applied, 'grid', axis=0, tiled=True)  50.9 us
    all_to_all x1, blocking collectives, sum_at_owner(): pieces = lax.all_to_all(in_blocks(shard, dim, size), axis, 0, 0, tiled=True)  38.8 us
    all_to_all x2, starting transfers between devices, sum_at_owner(): pieces = lax.all_to_all(in_blocks(shard, dim, size), axis, 0, 0, tiled=True)  18.2 us
  transfers between devices with their start and end apart: 7, of which 5 were waited for; matrix products, arithmetic and copies ran while one was open for 6% of the time, Pallas kernels for 0%

profile of v1, /device:TPU:8, one launch (start us, length us, event | category | flops | bytes accessed | tf_op | source)
XLA Modules:
  0.0 389.0 jit_solution(1158224936518430222)
XLA Ops:
  7.2 0.0 copy-start
  7.2 1.1 copy-done
  8.3 1.7 convolution_bitcast_fusion
  10.0 0.3 copy.25
  10.4 0.1 copy.26
  10.5 38.8 %all_to_all.38 = f32[8,2,64,256]{3,2,1,0:T(8,128)S(1)} all-to-all(f32[8,2,64,256]{3,2,1,0:T(8,128)S(1)} %copy.26), channel_id=1, replica_groups=mesh['dp'=8,'tensor'=4,'grid'=16] {'dp'}, dimensions={0} | all-to-all | bytes 2097152 | tf_op jit(solution)/shard_map/all_to_all | solution.py:28
  49.3 0.1 reduce_sum.27
  49.4 5.8 %all_gather.9 = bf16[2,64,1024]{2,1,0:T(8,128)(2,1)S(1)} all-gather(bf16[2,64,256]{2,1,0:T(8,128)(2,1)S(1)} %reduce_sum.27), channel_id=1, replica_groups=mesh['dp'=8,'tensor'=4,'grid'=16] {'tensor'}, dimensions={2}, use_global_device_ids=true | all-gather | bytes 327680 | tf_op jit(solution)/shard_map/all_gather | solution.py:51
  55.2 1.6 stack.2
  56.8 3.6 all-to-all-start.1
  60.4 0.0 reduce-scatter.2.cloned.1.call-start
  60.5 51.9 %all-to-all-done.1 = bf16[8,2,64,1024]{3,2,1,0:T(8,128)(2,1)S(1)} async-done(((bf16[8,2,64,1024]{3,2,1,0:T(8,128)(2,1)}), bf16[8,2,64,1024]{3,2,1,0:T(8,128)(2,1)S(1)}, u32[]{:S(2)}, u32[]{:S(2)}) %all-to-all-start.1) | async-done | bytes 2097184 | tf_op jit(solution)/shard_map/all_to_all | solution.py:13
  112.4 0.0 copy-start.1
  112.4 1.3 copy-done.1
  113.7 1.8 copy.27
  115.5 0.0 copy-start.2
  115.6 1.2 dynamic-slice_select_fusion
  116.7 0.0 reduce-scatter.2.cloned.1.call-update
  116.8 0.0 copy-done.2
  116.8 0.7 fusion.5
  117.5 1.4 copy.31
  118.9 8.8 %all-to-all-start.3 = ((f32[16,16,2,1024]{3,1,2,0:T(8,128)}), f32[16,16,2,1024]{3,1,2,0:T(8,128)}, u32[]{:S(2)}, u32[]{:S(2)}) async-start(f32[16,16,2,1024]{3,1,2,0:T(8,128)} %copy.31), calls=%async_computation.4 | async-start | bytes 4194304 | tf_op jit(solution)/shard_map/all_to_all | solution.py:28
  127.8 0.0 all-gather.3.cloned.1.call-start
  127.8 104.7 %reduce-scatter.2.cloned.1.call-done = bf16[32,1024]{1,0:T(8,128)(2,1)} async-done(((bf16[512,1024]{1,0:T(8,128)(2,1)}), bf16[32,1024]{1,0:T(8,128)(2,1)}) %reduce-scatter.2.cloned.1.call-update) | async-done | bytes 65552 | tf_op jit(solution)/shard_map/reduce_scatter | solution.py:44
  232.5 0.0 all-gather.3.cloned.1.call-update
  232.6 0.0 all-gather.5.cloned.1.call-start
  232.6 0.0 all-to-all-done.3
  232.6 2.4 reduce_sum.29
  235.0 0.0 all-gather.5.cloned.1.call-update
  235.0 57.0 %all-gather.3.cloned.1.call-done = bf16[512,1024]{1,0:T(8,128)(2,1)} async-done(((bf16[32,1024]{1,0:T(8,128)(2,1)}), bf16[512,1024]{1,0:T(8,128)(2,1)}) %all-gather.3.cloned.1.call-update) | async-done | bytes 1048592 | tf_op jit(solution)/shard_map/all_gather | solution.py:45
  292.0 1.8 fusion.2
  293.9 1.1 copy.30
  295.0 2.7 reshape.37
  297.6 9.3 %all-to-all-start.2 = ((f32[32,1,4096]{2,1,0:T(1,128)}), f32[32,1,4096]{2,1,0:T(1,128)S(1)}, u32[]{:S(2)}, u32[]{:S(2)}) async-start(f32[32,1,4096]{2,1,0:T(1,128)} %reshape.37), calls=%async_computation.3 | async-start | bytes 1048576 | tf_op jit(solution)/shard_map/all_to_all | solution.py:28
  307.0 50.9 %all-gather.5.cloned.1.call-done = f32[256,2,1024]{2,0,1:T(8,128)} async-done(((f32[16,2,1024]{2,0,1:T(8,128)}), f32[256,2,1024]{2,0,1:T(8,128)}) %all-gather.5.cloned.1.call-update) | async-done | bytes 2097168 | tf_op jit(solution)/shard_map/all_gather | solution.py:80
  357.9 2.8 convolution_bitcast_fusion.1
  360.6 0.8 copy.32
  361.5 1.9 reshape.39
  363.4 0.0 all-to-all-done.2
  363.4 6.7 %all-to-all-start.4 = ((f32[16,1,2048]{2,1,0:T(1,128)}), f32[16,1,2048]{2,1,0:T(1,128)S(1)}, u32[]{:S(2)}, u32[]{:S(2)}) async-start(f32[16,1,2048]{2,1,0:T(1,128)} %reshape.39), calls=%async_computation.5 | async-start | bytes 262144 | tf_op jit(solution)/shard_map/all_to_all | solution.py:85
  370.1 3.3 fusion
  373.4 0.0 copy-start.4
  373.4 0.5 broadcast.4
  373.9 1.9 reduce
  375.8 0.0 copy-start.3
  375.8 0.4 reshape.38
  376.2 0.1 reduce_sum.28
  376.3 0.0 copy-done.4
  376.3 0.6 multiply_add_fusion
  376.9 3.5 all-to-all-done.4
  380.5 0.9 reduce.1
  381.4 0.2 reshape.40
  381.6 0.1 copy.34
  381.7 0.1 all_to_all.32
  381.8 0.0 copy-done.3
  381.8 0.7 bitcast_add_fusion
  (1 shorter events, 0.0 us)
Async XLA Ops:
  7.2 1.1 copy-start
  56.8 55.6 %all-to-all-start.1 = ((bf16[8,2,64,1024]{3,2,1,0:T(8,128)(2,1)}), bf16[8,2,64,1024]{3,2,1,0:T(8,128)(2,1)S(1)}, u32[]{:S(2)}, u32[]{:S(2)}) async-start(bf16[8,2,64,1024]{3,2,1,0:T(8,128)(2,1)} %stack.2), calls=%async_computation.1 | async-start | bytes 4194304 | tf_op jit(solution)/shard_map/all_to_all | solution.py:13
  60.4 172.2 %reduce-scatter.2.cloned.1.call-start = ((), (), s32[]{:S(2)}) async-start(), calls=%async_computation.6 | async-start | bytes 1114112 | tf_op jit(solution)/shard_map/reduce_scatter | solution.py:44
  112.4 1.3 copy-start.1
  115.5 1.2 copy-start.2
  118.9 113.7 %all-to-all-start.3 = ((f32[16,16,2,1024]{3,1,2,0:T(8,128)}), f32[16,16,2,1024]{3,1,2,0:T(8,128)}, u32[]{:S(2)}, u32[]{:S(2)}) async-start(f32[16,16,2,1024]{3,1,2,0:T(8,128)} %copy.31), calls=%async_computation.4 | async-start | bytes 4194304 | tf_op jit(solution)/shard_map/all_to_all | solution.py:28
  127.8 164.3 %all-gather.3.cloned.1.call-start = ((), (), s32[]{:S(2)}) async-start(), calls=%async_computation.7 | async-start | bytes 1114112 | tf_op jit(solution)/shard_map/all_gather | solution.py:45
  232.6 125.3 %all-gather.5.cloned.1.call-start = ((), (), s32[]{:S(2)}) async-start(), calls=%async_computation.8 | async-start | bytes 2228224 | tf_op jit(solution)/shard_map/all_gather | solution.py:80
  297.6 65.7 %all-to-all-start.2 = ((f32[32,1,4096]{2,1,0:T(1,128)}), f32[32,1,4096]{2,1,0:T(1,128)S(1)}, u32[]{:S(2)}, u32[]{:S(2)}) async-start(f32[32,1,4096]{2,1,0:T(1,128)} %reshape.37), calls=%async_computation.3 | async-start | bytes 1048576 | tf_op jit(solution)/shard_map/all_to_all | solution.py:28
  363.4 17.1 %all-to-all-start.4 = ((f32[16,1,2048]{2,1,0:T(1,128)}), f32[16,1,2048]{2,1,0:T(1,128)S(1)}, u32[]{:S(2)}, u32[]{:S(2)}) async-start(f32[16,1,2048]{2,1,0:T(1,128)} %reshape.39), calls=%async_computation.5 | async-start | bytes 262144 | tf_op jit(solution)/shard_map/all_to_all | solution.py:85
  373.4 2.9 copy-start.4
  375.8 6.1 %copy-start.3 = (f32[2,16,1024]{2,1,0:T(8,128)S(1)}, f32[2,16,1024]{2,1,0:T(8,128)}, u32[]{:S(2)}) copy-start(f32[2,16,1024]{2,1,0:T(8,128)} %param.13) | copy-start | bytes 393220
Sparse Core Ops, SparseCore 0:
  116.9 115.6 reduce-scatter.1
  236.0 56.0 all-gather.2
  296.1 61.7 all-gather.4
